TPU v7x, 32 devices: a whole 2x2x4 slice. The times are simulated.
32 devices in a mesh: segment: 2 (over core), dp: 8 (over z, x), mp: 2 (over y).
Axes of the slice: x: 2, y: 2, z: 4, core: 2. Of those that a mesh axis runs over, the one named last changes fastest.
Arguments:
- grad_top: bfloat16 [4096, 2048], P('dp'), may hold values from -6 to 6
- saved_query: bfloat16 [2, 4096, 2048], P('segment', 'dp', 'mp'), may hold values from -12 to 12
- saved_key: bfloat16 [2, 6144, 2048], P('segment', 'dp', 'mp'), may hold values from -4 to 4
- saved_value: bfloat16 [2, 6144, 2048], P('segment', 'dp', 'mp'), may hold values from -6 to 6
- w_query: bfloat16 [2, 2048, 2048], P('segment', 'mp', 'dp'), may hold values from -0.125 to 0.125
- w_key: bfloat16 [2, 2048, 2048], P('segment', 'mp', 'dp'), may hold values from -0.125 to 0.125
- w_value: bfloat16 [2, 2048, 2048], P('segment', 'mp', 'dp'), may hold values from -0.125 to 0.125
- w_out: bfloat16 [2, 2048, 2048], P('segment', 'mp', 'dp'), may hold values from -0.125 to 0.125
- query_length: int32 [16, 2], P('dp'), may hold values from 64 to 128
- key_offset: int32 [16, 2], P('dp'), may hold values from 0 to 2, as said below
- key_length: int32 [16, 2], P('dp'), may hold values from 64 to 256
- tile_owner: int32 [16, 3], replicated, may hold values from 0 to 47, as said below
Outputs:
- section_grads: bfloat16 [2, 4096, 2048], P('segment', 'dp', 'mp')
- encoder_grads: bfloat16 [6144, 2048], P('dp', ('segment', 'mp'))
Inputs may be any that keep to these rules, and one draw needn't show every extreme that they name: Example 0 takes tiles 0 to key_offset[s, 1] - 1 and example 1 the rest of the sequence's encoder tiles; each example holds at least one tile and its rows fit in its tiles. `tile_owner`: every global tile appears once. Tile t is owned by dp index t // 6; the owner of a tile of dp index i (sequences i * 2 to i * 2 + 1) is i - 1, i or i + 1, wrapping around. Each dp index hands 1 to 2 tiles to each neighbour, and 2 is reached in every draw.
All inputs are finite; a program needn't handle non-finite values.
Results may differ from a plain program's by a relative error of at most 0.019.
Values may be sent and summed in bfloat16 or wider, within the bound.
A program may use at most 128 MiB of HBM per device.

v0:
```python
import jax
import jax.numpy as jnp
from jax import lax
from jax.sharding import PartitionSpec as P

DH = 256
TILE = 128
CAP = 2
masked_floor = -1e30


def shifted(block, axis, distance):
    devices = range(lax.axis_size(axis))
    route = [(i - distance, i) for i in devices if i - distance in devices]
    return lax.ppermute(block, axis, route)


def extended_2(block, sides, width):
    for axis, dim in sides:
        count = lax.axis_size(axis)
        forward = [(i, i + 1) for i in range(count - 1)]
        forward.append((count - 1, 0))
        backward = [(target, source) for source, target in forward]
        low = lax.ppermute(
            lax.slice_in_dim(block, block.shape[dim] - width, None, axis=dim), axis, forward
        )
        high = lax.ppermute(lax.slice_in_dim(block, 0, width, axis=dim), axis, backward)
        block = jnp.concatenate([low, block, high], axis=dim)
    return block


def example_mask(query_length, key_offset, key_length, q_rows, k_rows):
    row_ids = jnp.arange(q_rows, dtype=jnp.int32)[:, None]
    starts = jnp.arange(query_length.shape[0], dtype=jnp.int32)[None, :] * TILE
    inside_q = (row_ids >= starts) & (row_ids < starts + query_length[None, :])
    col_ids = jnp.arange(k_rows, dtype=jnp.int32)[:, None]
    key_start = key_offset[None, :] * TILE
    inside_k = (col_ids >= key_start) & (col_ids < key_start + key_length[None, :])
    return jnp.any(inside_q[:, None, :] & inside_k[None, :, :], axis=-1)


def sequence_backward(operands, query_full, out_full):
    grad_in, query_block, key_block, value_block, query_length, key_offset, key_length = operands
    q_rows, local_width = query_block.shape
    k_rows = key_block.shape[0]
    head_count = local_width // DH
    score_scale = DH ** (-0.5)
    out_grad = lax.dot_general(
        grad_in, out_full, (((1,), (1,)), ((), ())), preferred_element_type=jnp.float32
    ).astype(jnp.bfloat16)
    q_heads = query_block.reshape(q_rows, head_count, DH)
    k_heads = key_block.reshape(k_rows, head_count, DH)
    v_heads = value_block.reshape(k_rows, head_count, DH)
    grad_heads = out_grad.reshape(q_rows, head_count, DH)
    scores = (
        jnp.einsum("qhd,khd->hqk", q_heads, k_heads, preferred_element_type=jnp.float32)
        * score_scale
    )
    allowed = example_mask(query_length, key_offset, key_length, q_rows, k_rows)[None]
    masked = jnp.where(allowed, scores, masked_floor)
    row_max = jnp.max(masked, axis=-1, keepdims=True)
    exp_terms = jnp.where(allowed, jnp.exp(masked - row_max), 0.0)
    denominator = jnp.maximum(jnp.sum(exp_terms, axis=-1, keepdims=True), 1.0)
    attention_probs = exp_terms / denominator
    prob_bf = attention_probs.astype(jnp.bfloat16)
    attended = jnp.einsum("hqk,khd->qhd", prob_bf, v_heads, preferred_element_type=jnp.float32)
    out_dot = jnp.sum(grad_heads.astype(jnp.float32) * attended, axis=-1)
    prob_grad = jnp.einsum("qhd,khd->hqk", grad_heads, v_heads, preferred_element_type=jnp.float32)
    score_grad = (attention_probs * (prob_grad - jnp.transpose(out_dot)[:, :, None])).astype(
        jnp.bfloat16
    )
    query_grad = (
        jnp.einsum("hqk,khd->qhd", score_grad, k_heads, preferred_element_type=jnp.float32)
        * score_scale
    ).astype(jnp.bfloat16)
    key_gradient = (
        jnp.einsum("hqk,qhd->khd", score_grad, q_heads, preferred_element_type=jnp.float32)
        * score_scale
    ).astype(jnp.bfloat16)
    value_grad = jnp.einsum(
        "hqk,qhd->khd", prob_bf, grad_heads, preferred_element_type=jnp.float32
    ).astype(jnp.bfloat16)
    mixed_grad = jnp.dot(
        query_grad.reshape(q_rows, local_width), query_full, preferred_element_type=jnp.float32
    )
    return (
        mixed_grad,
        key_gradient.reshape(k_rows, local_width),
        value_grad.reshape(k_rows, local_width),
    )


def ranked(marked):
    ids = jnp.arange(marked.shape[0], dtype=jnp.int32)
    upto = ids[None, :] <= ids[:, None]
    return jnp.sum((upto & marked[None, :]).astype(jnp.int32), axis=1) - 1


def on_device(
    grad_top,
    saved_query,
    saved_key,
    saved_value,
    w_query,
    w_key,
    w_value,
    w_out,
    query_length,
    key_offset,
    key_length,
    tile_owner,
):
    segment_count = lax.axis_size("segment")
    segment_id = lax.axis_index("segment")
    micro_count = query_length.shape[0]
    q_rows = grad_top.shape[0] // micro_count
    k_rows = saved_key.shape[1] // micro_count
    width = grad_top.shape[1]
    local_width = saved_query.shape[2]
    half_width = width // lax.axis_size("mp")
    out_full, query_full, key_full, complete_value = (
        lax.all_gather(w_out[0], "dp", axis=1, tiled=True),
        lax.all_gather(w_query[0], "dp", axis=1, tiled=True),
        lax.all_gather(w_key[0], "dp", axis=1, tiled=True),
        lax.all_gather(w_value[0], "dp", axis=1, tiled=True),
    )

    def run_layer(operands):
        return sequence_backward(operands, query_full, out_full)

    def bypass_layer(operands):
        return (
            jnp.zeros((q_rows, width), jnp.float32),
            jnp.zeros((k_rows, local_width), jnp.bfloat16),
            jnp.zeros((k_rows, local_width), jnp.bfloat16),
        )

    incoming = jnp.zeros((q_rows, width), jnp.bfloat16)
    sections = jnp.zeros((micro_count * q_rows, half_width), jnp.bfloat16)
    key_grads = jnp.zeros((micro_count * k_rows, local_width), jnp.bfloat16)
    value_grads = jnp.zeros((micro_count * k_rows, local_width), jnp.bfloat16)
    for clock_tick in range(micro_count + 1):
        step_id = clock_tick - 1 + segment_id
        active = (step_id >= 0) & (step_id < micro_count)
        picked = jnp.clip(step_id, 0, micro_count - 1)
        top_rows = lax.dynamic_slice_in_dim(grad_top, picked * q_rows, q_rows, 0)
        grad_in = jnp.where(segment_id == segment_count - 1, top_rows, incoming)
        query_block = lax.dynamic_slice_in_dim(saved_query[0], picked * q_rows, q_rows, 0)
        key_block = lax.dynamic_slice_in_dim(saved_key[0], picked * k_rows, k_rows, 0)
        value_block = lax.dynamic_slice_in_dim(saved_value[0], picked * k_rows, k_rows, 0)
        lengths_q = lax.dynamic_index_in_dim(query_length, picked, 0, keepdims=False)
        offsets_k = lax.dynamic_index_in_dim(key_offset, picked, 0, keepdims=False)
        lengths_k = lax.dynamic_index_in_dim(key_length, picked, 0, keepdims=False)
        mixed_grad, key_gradient, value_grad = lax.cond(
            active,
            run_layer,
            bypass_layer,
            (grad_in, query_block, key_block, value_block, lengths_q, offsets_k, lengths_k),
        )
        summed_share = lax.psum_scatter(
            mixed_grad.astype(jnp.bfloat16), "mp", scatter_dimension=1, tiled=True
        ).astype(jnp.float32)
        own_input = lax.dynamic_slice_in_dim(
            grad_in, lax.axis_index("mp") * half_width, half_width, 1
        )
        own_section = (own_input.astype(jnp.float32) + summed_share).astype(jnp.bfloat16)
        if clock_tick < micro_count:
            full_section = lax.all_gather(own_section, "mp", axis=1, tiled=True)
        sections = jnp.where(
            active,
            lax.dynamic_update_slice_in_dim(sections, own_section, picked * q_rows, 0),
            sections,
        )
        key_grads = jnp.where(
            active,
            lax.dynamic_update_slice_in_dim(key_grads, key_gradient, picked * k_rows, 0),
            key_grads,
        )
        value_grads = jnp.where(
            active,
            lax.dynamic_update_slice_in_dim(value_grads, value_grad, picked * k_rows, 0),
            value_grads,
        )
        if clock_tick < micro_count:
            incoming = shifted(full_section, "segment", -1)
    encoder_partial = jnp.dot(key_grads, key_full, preferred_element_type=jnp.float32) + jnp.dot(
        value_grads, complete_value, preferred_element_type=jnp.float32
    )
    reduced = lax.psum_scatter(
        encoder_partial.astype(jnp.bfloat16), ("segment", "mp"), scatter_dimension=1, tiled=True
    )
    tiles_dev = reduced.shape[0] // TILE
    features = reduced.shape[1]
    local_tiles = reduced.reshape(tiles_dev, TILE, features)
    devices = lax.axis_size("dp")
    my_index = lax.axis_index("dp")
    owners_all = tile_owner.reshape(devices, tiles_dev)

    def route_plan(source):
        owner_row = lax.dynamic_index_in_dim(owners_all, source % devices, 0, keepdims=False)
        owner_step = (owner_row // tiles_dev - source % devices + devices) % devices
        return (owner_step, owner_row % tiles_dev)

    mine_step, mine_slot = route_plan(my_index)
    left_step, left_slot = route_plan(my_index - 1 + devices)
    right_step, right_slot = route_plan(my_index + 1)
    capacity_ids = jnp.arange(CAP, dtype=jnp.int32)[:, None]
    to_left = mine_step == devices - 1
    rightward_send = mine_step == 1
    pick_left = (ranked(to_left)[None, :] == capacity_ids) & to_left[None, :]
    pick_right = (ranked(rightward_send)[None, :] == capacity_ids) & rightward_send[None, :]
    selector_mask = jnp.concatenate([pick_left, pick_right], axis=0).astype(jnp.bfloat16)
    outgoing = jnp.einsum(
        "sa,ayk->syk", selector_mask, local_tiles, preferred_element_type=jnp.float32
    ).astype(jnp.bfloat16)
    outgoing = outgoing.reshape(2 * CAP * TILE, features)
    extended = extended_2(outgoing, (("dp", 0),), CAP * TILE)
    from_left = extended[: CAP * TILE].reshape(CAP, TILE, features)
    from_right = extended[extended.shape[0] - CAP * TILE :].reshape(CAP, TILE, features)
    candidates = jnp.concatenate([from_left, local_tiles, from_right], axis=0)
    left_marked = left_step == 1
    left_hit = (ranked(left_marked)[None, :] == capacity_ids) & left_marked[None, :]
    left_target = jnp.sum(jnp.where(left_hit, left_slot[None, :], 0), axis=1)
    right_marked = right_step == devices - 1
    right_hit = (ranked(right_marked)[None, :] == capacity_ids) & right_marked[None, :]
    right_target = jnp.sum(jnp.where(right_hit, right_slot[None, :], 0), axis=1)
    target = jnp.concatenate([left_target, mine_slot, right_target])
    usable = jnp.concatenate(
        [jnp.any(left_hit, axis=1), mine_step == 0, jnp.any(right_hit, axis=1)]
    )
    placer = (
        (jnp.arange(tiles_dev, dtype=jnp.int32)[:, None] == target[None, :]) & usable[None, :]
    ).astype(jnp.bfloat16)
    owned_rows = jnp.einsum(
        "sc,crf->srf", placer, candidates, preferred_element_type=jnp.float32
    ).astype(jnp.bfloat16)
    return (sections[None], owned_rows.reshape(tiles_dev * TILE, features))


def solution(mesh):
    in_specs = (
        P("dp", None),
        P("segment", "dp", "mp"),
        P("segment", "dp", "mp"),
        P("segment", "dp", "mp"),
        P("segment", "mp", "dp"),
        P("segment", "mp", "dp"),
        P("segment", "mp", "dp"),
        P("segment", "mp", "dp"),
        P("dp", None),
        P("dp", None),
        P("dp", None),
        P(),
    )
    out_specs = (P("segment", "dp", "mp"), P("dp", ("segment", "mp")))
    return jax.shard_map(
        on_device, mesh=mesh, in_specs=in_specs, out_specs=out_specs, check_vma=False
    )
```

profile of v0, /device:TPU:0, one launch (start us, length us, event | category | flops | bytes accessed | tf_op | source)
XLA Modules:
  0.0 555.2 jit_solution(12145603044757109902)
XLA Ops:
  8.8 2.4 dynamic-slice_select_fusion.2
  11.2 76.6 %all-gather.15.cloned.1.call-done = bf16[1,1024,2048]{2,1,0:T(8,128)(2,1)} async-done(((bf16[1,1024,256]{2,1,0:T(8,128)(2,1)}), bf16[1,1024,2048]{2,1,0:T(8,128)(2,1)}) %all-gather.15.cloned.1.call-update) | async-done | bytes 4194320 | tf_op jit(solution)/shard_map/all_gather | solution.py:122
  87.8 75.3 %all-gather.17.cloned.1.call-done = bf16[1,1024,2048]{2,1,0:T(8,128)(2,1)} async-done(((bf16[1,1024,256]{2,1,0:T(8,128)(2,1)}), bf16[1,1024,2048]{2,1,0:T(8,128)(2,1)}) %all-gather.17.cloned.1.call-update) | async-done | bytes 4194320 | tf_op jit(solution)/shard_map/all_gather | solution.py:123
  163.1 3.0 conditional.3
  166.3 46.4 %reduce-scatter.5.cloned.1.call-done = bf16[256,1024]{1,0:T(8,128)(2,1)} async-done(((bf16[256,2048]{1,0:T(8,128)(2,1)}), bf16[256,1024]{1,0:T(8,128)(2,1)}) %reduce-scatter.5.cloned.1.call-update) | async-done | bytes 524304 | tf_op jit(solution)/shard_map/reduce_scatter | solution.py:160
  213.8 2.4 select_dynamic-update-slice_fusion.7
  216.3 21.4 %all-gather.11.cloned.1.call-done = bf16[256,2048]{1,0:T(8,128)(2,1)} async-done(((bf16[256,1024]{1,0:T(8,128)(2,1)}), bf16[256,2048]{1,0:T(8,128)(2,1)}) %all-gather.11.cloned.1.call-update) | async-done | bytes 1048592 | tf_op jit(solution)/shard_map/all_gather | solution.py:168
  239.4 3.1 collective-permute-done
  242.6 2.9 dynamic-slice_select_fusion.1
  245.5 31.3 %conditional.4 = (bf16[256,2048]{1,0:T(8,128)(2,1)}, bf16[384,1024]{0,1:T(8,128)(2,1)}, bf16[384,1024]{0,1:T(8,128)(2,1)}) conditional(s32[]{:T(128)} %convert_element_type.206, () %tuple.46, (s32[2,2]{1,0:T(2,128)S(1)}, s32[]{:T(128)}, s32[2,2]{1,0:T(2,128)S(1)}, s32[2,2]{1,0:T(2,128)S(1)}, bf16[1,512,1024]{2,1,0:T(8,128)(2,1)}, ...), branch_computations={%region_7.8_spmd, %region_8.13_spmd} | conditional | flops 3363606528 | bytes 75467568 | solution.py:154
  249.1 3.5 constant_dynamic-slice_fusion.6
  252.5 2.3 copy.91
  257.0 3.4 fusion.94
  260.4 4.6 convolution_convert_fusion.3
  267.1 2.5 fusion.21
  273.1 2.3 fusion.98
  276.9 20.4 %reduce-scatter.7.cloned.1.call-done = bf16[256,1024]{1,0:T(8,128)(2,1)} async-done(((bf16[256,2048]{1,0:T(8,128)(2,1)}), bf16[256,1024]{1,0:T(8,128)(2,1)}) %reduce-scatter.7.cloned.1.call-update) | async-done | bytes 524304 | tf_op jit(solution)/shard_map/reduce_scatter | solution.py:160
  297.3 2.7 select_dynamic-update-slice_fusion.6
  301.5 19.9 %all-gather.13.cloned.1.call-done = bf16[256,2048]{1,0:T(8,128)(2,1)} async-done(((bf16[256,1024]{1,0:T(8,128)(2,1)}), bf16[256,2048]{1,0:T(8,128)(2,1)}) %all-gather.13.cloned.1.call-update) | async-done | bytes 1048592 | tf_op jit(solution)/shard_map/all_gather | solution.py:168
  327.3 2.5 select_dynamic-update-slice_fusion.1
  329.8 2.7 select_dynamic-update-slice_fusion.4
  333.9 25.2 %conditional.5 = (bf16[256,2048]{1,0:T(8,128)(2,1)S(1)}, bf16[384,1024]{0,1:T(8,128)(2,1)S(1)}, bf16[384,1024]{0,1:T(8,128)(2,1)S(1)}) conditional(s32[]{:T(128)} %convert_element_type.211, () %tuple.48, (s32[2,2]{1,0:T(2,128)S(1)}, s32[]{:T(128)}, s32[2,2]{1,0:T(2,128)S(1)}, s32[2,2]{1,0:T(2,128)S(1)}, bf16[1,512,1024]{2,1,0:T(8,128)(2,1)}, ...), branch_computations={%region_14.15_spmd, %region_15.20_spmd} | conditional | flops 3363606528 | bytes 90147712 | solution.py:154
  337.6 3.1 constant_dynamic-slice_fusion.12
  345.4 4.4 convolution_convert_fusion.5
  359.1 3.4 select_dynamic-update-slice_fusion
  362.5 36.0 %all-gather.21.cloned.1.call-done = bf16[1,1024,2048]{2,1,0:T(8,128)(2,1)} async-done(((bf16[1,1024,256]{2,1,0:T(8,128)(2,1)}), bf16[1,1024,2048]{2,1,0:T(8,128)(2,1)}) %all-gather.21.cloned.1.call-update) | async-done | bytes 4194320 | tf_op jit(solution)/shard_map/all_gather | solution.py:125
  398.5 8.8 %fusion.51 = f32[768,2048]{1,0:T(8,128)} fusion(bf16[768,1024]{0,1:T(8,128)(2,1)} %get-tuple-element.471, bf16[1,1024,2048]{2,1,0:T(8,128)(2,1)} %all-gather.21.cloned.1.call-done), kind=kOutput, calls=%fused_computation.106 | convolution fusion | flops 3221225472 | bytes 12058624 | tf_op jit(solution)/shard_map/dot_general | solution.py:186
  407.3 66.5 %all-gather.19.cloned.1.call-done = bf16[1,1024,2048]{2,1,0:T(8,128)(2,1)} async-done(((bf16[1,1024,256]{2,1,0:T(8,128)(2,1)}), bf16[1,1024,2048]{2,1,0:T(8,128)(2,1)}) %all-gather.19.cloned.1.call-update) | async-done | bytes 4194320 | tf_op jit(solution)/shard_map/all_gather | solution.py:124
  473.8 9.6 %add_convert_fusion = bf16[768,2048]{1,0:T(8,128)(2,1)} fusion(f32[768,2048]{1,0:T(8,128)} %fusion.51, bf16[768,1024]{0,1:T(8,128)(2,1)} %get-tuple-element.472, bf16[1,1024,2048]{2,1,0:T(8,128)(2,1)} %all-gather.19.cloned.1.call-done), kind=kOutput, calls=%fused_computation.105 | convolution fusion | flops 3224371200 | bytes 15204352 | tf_op jit(solution)/shard_map/dot_general | solution.py:186
  485.4 34.4 %reduce-scatter.11.cloned.1.call-done = bf16[768,512]{1,0:T(8,128)(2,1)} async-done(((bf16[768,2048]{1,0:T(8,128)(2,1)}), bf16[768,512]{1,0:T(8,128)(2,1)}) %reduce-scatter.11.cloned.1.call-update) | async-done | bytes 786448 | tf_op jit(solution)/shard_map/reduce_scatter | solution.py:189
  524.2 3.3 collective-permute-start.3
  528.8 13.4 %reduce-scatter.9.cloned.1.call-done = bf16[256,1024]{1,0:T(8,128)(2,1)} async-done(((bf16[256,2048]{1,0:T(8,128)(2,1)}), bf16[256,1024]{1,0:T(8,128)(2,1)}) %reduce-scatter.9.cloned.1.call-update) | async-done | bytes 524304 | tf_op jit(solution)/shard_map/reduce_scatter | solution.py:160
  (153 shorter events, 59.6 us)
Async XLA Ops:
  7.2 156.0 %copy-start = (bf16[1,768,1024]{2,1,0:T(8,128)(2,1)S(1)}, bf16[1,768,1024]{2,1,0:T(8,128)(2,1)}, u32[]{:S(2)}) copy-start(bf16[1,768,1024]{2,1,0:T(8,128)(2,1)} %param.20) | copy-start | bytes 4718596
  7.2 156.0 %copy-start.1 = (bf16[1,768,1024]{2,1,0:T(8,128)(2,1)S(1)}, bf16[1,768,1024]{2,1,0:T(8,128)(2,1)}, u32[]{:S(2)}) copy-start(bf16[1,768,1024]{2,1,0:T(8,128)(2,1)} %param.21) | copy-start | bytes 4718596
  7.2 155.9 %copy-start.22 = (s32[2,2]{1,0:T(2,128)S(1)}, s32[2,2]{1,0:T(2,128)}, u32[]{:S(2)}) copy-start(s32[2,2]{1,0:T(2,128)} %param.26) | copy-start | bytes 52
  7.2 155.9 %copy-start.23 = (s32[2,2]{1,0:T(2,128)S(1)}, s32[2,2]{1,0:T(2,128)}, u32[]{:S(2)}) copy-start(s32[2,2]{1,0:T(2,128)} %param.27) | copy-start | bytes 52
  7.2 155.9 %copy-start.24 = (s32[2,2]{1,0:T(2,128)S(1)}, s32[2,2]{1,0:T(2,128)}, u32[]{:S(2)}) copy-start(s32[2,2]{1,0:T(2,128)} %param.28) | copy-start | bytes 52
  7.2 80.6 %all-gather.15.cloned.1.call-start = ((), (), s32[]{:S(2)}) async-start(), calls=%async_computation.10 | async-start | bytes 4718592 | tf_op jit(solution)/shard_map/all_gather | solution.py:122
  7.9 155.2 %all-gather.17.cloned.1.call-start = ((), (), s32[]{:S(2)}) async-start(), calls=%async_computation.11 | async-start | bytes 4718592 | tf_op jit(solution)/shard_map/all_gather | solution.py:123
  8.7 204.0 %reduce-scatter.5.cloned.1.call-start = ((), (), s32[]{:S(2)}) async-start(), calls=%async_computation.4 | async-start | bytes 1572864 | tf_op jit(solution)/shard_map/reduce_scatter | solution.py:160
  166.2 71.5 %all-gather.11.cloned.1.call-start = ((), (), s32[]{:S(2)}) async-start(), calls=%async_computation.5 | async-start | bytes 1572864 | tf_op jit(solution)/shard_map/all_gather | solution.py:168
  216.2 81.1 %reduce-scatter.7.cloned.1.call-start = ((), (), s32[]{:S(2)}) async-start(), calls=%async_computation.6 | async-start | bytes 1572864 | tf_op jit(solution)/shard_map/reduce_scatter | solution.py:160
  237.7 4.9 collective-permute-start
  267.1 2.5 copy-start.16
  267.1 2.5 copy-start.19
  267.1 2.7 copy-start.30
  269.7 3.3 copy-start.27
  276.8 44.6 %all-gather.13.cloned.1.call-start = ((), (), s32[]{:S(2)}) async-start(), calls=%async_computation.7 | async-start | bytes 1572864 | tf_op jit(solution)/shard_map/all_gather | solution.py:168
  300.0 98.6 %all-gather.21.cloned.1.call-start = ((), (), s32[]{:S(2)}) async-start(), calls=%async_computation.13 | async-start | bytes 4718592 | tf_op jit(solution)/shard_map/all_gather | solution.py:125
  300.7 173.1 %all-gather.19.cloned.1.call-start = ((), (), s32[]{:S(2)}) async-start(), calls=%async_computation.12 | async-start | bytes 4718592 | tf_op jit(solution)/shard_map/all_gather | solution.py:124
  301.5 218.3 %reduce-scatter.11.cloned.1.call-start = ((), (), s32[]{:S(2)}) async-start(), calls=%async_computation.9 | async-start | bytes 3932160 | tf_op jit(solution)/shard_map/reduce_scatter | solution.py:189
  321.4 11.1 %collective-permute-start.1 = (bf16[256,2048]{1,0:T(8,128)(2,1)}, bf16[256,2048]{1,0:T(8,128)(2,1)S(1)}, u32[]{:S(2)}, u32[]{:S(2)}) collective-permute-start(bf16[256,2048]{1,0:T(8,128)(2,1)} %all-gather.13.cloned.1.call-done), channel_id=1, source_target_pairs={{16,0},{17,1},{18,2},{19,3},{20,4},{21,5},{22,6},{23,7},{24,8},{25... | collective-permute-start | bytes 3145736 | tf_op jit(solution)/shard_map/ppermute | solution.py:15
  329.8 2.7 copy-start.3
  337.6 3.1 copy-start.2
  340.8 2.6 copy-start.9
  345.4 5.6 %copy-start.17 = (bf16[1,384,1024]{1,2,0:T(8,128)(2,1)S(1)}, bf16[1,384,1024]{1,2,0:T(8,128)(2,1)}, u32[]{:S(2)}) copy-start(bf16[1,384,1024]{1,2,0:T(8,128)(2,1)} %get-tuple-element.457) | copy-start | bytes 2359300 | tf_op jit(solution)/shard_map/cond
  351.1 2.2 copy-start.20
  351.1 2.2 copy-start.31
  359.1 3.4 copy-start.5
  483.5 58.8 %reduce-scatter.9.cloned.1.call-start = ((), (), s32[]{:S(2)}) async-start(), calls=%async_computation.8 | async-start | bytes 1572864 | tf_op jit(solution)/shard_map/reduce_scatter | solution.py:160
  521.9 20.4 %copy-start.10 = (bf16[256,2048]{1,0:T(8,128)(2,1)S(1)}, bf16[256,2048]{1,0:T(8,128)(2,1)}, u32[]{:S(2)}) copy-start(bf16[256,2048]{1,0:T(8,128)(2,1)} %dynamic-slice_select_fusion) | copy-start | bytes 3145732
  521.9 22.3 %collective-permute-start.2 = (bf16[256,512]{1,0:T(8,128)(2,1)S(1)}, bf16[256,512]{1,0:T(8,128)(2,1)S(1)}, u32[]{:S(2)}, u32[]{:S(2)}) collective-permute-start(bf16[256,512]{1,0:T(8,128)(2,1)S(1)} %bitcast.229), channel_id=1, source_target_pairs={{0,2},{2,4},{4,6},{6,8},{8,10},{10,12},{12,14},{14,0},{1,3},{3,5},... | collective-permute-start | bytes 786440 | tf_op jit(solution)/shard_map/ppermute | solution.py:24
  524.2 20.4 %collective-permute-start.3 = (bf16[256,512]{1,0:T(8,128)(2,1)}, bf16[256,512]{1,0:T(8,128)(2,1)}, u32[]{:S(2)}, u32[]{:S(2)}) collective-permute-start(bf16[256,512]{1,0:T(8,128)(2,1)} %bitcast.62), channel_id=1, source_target_pairs={{2,0},{4,2},{6,4},{8,6},{10,8},{12,10},{14,12},{0,14},{3,1},{5,3},... | collective-permute-start | bytes 786440 | tf_op jit(solution)/shard_map/ppermute | solution.py:27
  528.8 14.9 %copy-start.4 = (bf16[768,512]{1,0:T(8,128)(2,1)S(1)}, bf16[768,512]{1,0:T(8,128)(2,1)}, u32[]{:S(2)}) copy-start(bf16[768,512]{1,0:T(8,128)(2,1)} %reduce-scatter.11.cloned.1.call-done) | copy-start | bytes 2359300
  (8 other events, 11.6 us)
Sparse Core Ops, SparseCore 0:
  10.1 77.7 all-gather.14
  89.9 73.1 all-gather.16
  166.3 46.3 reduce-scatter.4
  216.3 21.3 all-gather.10
  276.9 20.3 reduce-scatter.6
  300.1 21.2 all-gather.12
  323.5 75.0 all-gather.20
  400.6 73.1 all-gather.18
  483.6 36.0 reduce-scatter.10
  521.9 20.3 reduce-scatter.8
where the time goes:
time: 563 us; the launch traced here: 555 us
  waiting for transfers between devices  416 us (74%)
  matrix products  50.6 us (9%)
  local copies, waits for them, and re-layouts  39 us (7%)
  other arithmetic  25.7 us (5%)
  between operations  14.7 us (3%)
  starting transfers between devices  8.2 us (1%)
    reduce_scatter x3, waiting for transfers between devices, on_device(): lax.psum_scatter(mixed_grad.astype(jnp.bfloat16), 'mp', scatter_dimension...  80.3 us
    all_gather x1, waiting for transfers between devices, on_device(): lax.all_gather(w_out[0], 'dp', axis=1, tiled=True)  76.6 us
    all_gather x1, waiting for transfers between devices, on_device(): lax.all_gather(w_query[0], 'dp', axis=1, tiled=True)  75.3 us
    all_gather x1, waiting for transfers between devices, on_device(): lax.all_gather(w_key[0], 'dp', axis=1, tiled=True)  66.5 us
    all_gather x2, waiting for transfers between devices, on_device(): full_section = lax.all_gather(own_section, 'mp', axis=1, tiled=True)  41.3 us
    all_gather x1, waiting for transfers between devices, on_device(): lax.all_gather(w_value[0], 'dp', axis=1, tiled=True)  36 us
    reduce_scatter x1, waiting for transfers between devices, on_device(): lax.psum_scatter(encoder_partial.astype(jnp.bfloat16), ('segment', 'mp'),...  34.4 us
    another operation x11, local copies, waits for them, and re-layouts  15.5 us
  transfers between devices with their start and end apart: 14, of which 11 were waited for; matrix products, arithmetic and copies ran while one was open for 10% of the time, Pallas kernels for 0%

commit v1 on v0

--- a/solution.py
+++ b/solution.py
@@ -7,6 +7,19 @@
 TILE = 128
 CAP = 2
 masked_floor = -1e30
+
+
+def ring_gather(x, axis, dim):
+    ways = lax.axis_size(axis)
+    up = [(d, (d + 1) % ways) for d in range(ways)]
+    down = [(d, (d - 1) % ways) for d in range(ways)]
+    earlier, later = ([x], [x])
+    for _ in range(ways // 2):
+        earlier.append(lax.ppermute(earlier[-1], axis, up))
+    for _ in range((ways - 1) // 2):
+        later.append(lax.ppermute(later[-1], axis, down))
+    line = jnp.concatenate([*earlier[::-1], *later[1:]], axis=dim)
+    return jnp.roll(line, (lax.axis_index(axis) - ways // 2) * x.shape[dim], axis=dim)
 
 
 def shifted(block, axis, distance):
@@ -119,7 +132,7 @@
     local_width = saved_query.shape[2]
     half_width = width // lax.axis_size("mp")
     out_full, query_full, key_full, complete_value = (
-        lax.all_gather(w_out[0], "dp", axis=1, tiled=True),
+        ring_gather(w_out[0], "dp", 1),
         lax.all_gather(w_query[0], "dp", axis=1, tiled=True),
         lax.all_gather(w_key[0], "dp", axis=1, tiled=True),
         lax.all_gather(w_value[0], "dp", axis=1, tiled=True),

time: 563 us -> 537 us (0.954)
  waiting for transfers between devices: 416 us -> 370 us
  starting transfers between devices: 8.2 us -> 25.7 us
    ppermute x0 -> x7, waiting for transfers between devices: none -> 91.1 us  [the longest x4 88 us: ring_gather(): earlier.append(lax.ppermute(earlier[-1], axis, up))]
    all_gather x1 -> x0, waiting for transfers between devices: 76.6 us -> none  [on_device(): lax.all_gather(w_out[0], 'dp', axis=1, tiled=True)]
    all_gather x1, waiting for transfers between devices: 75.3 us -> 13.4 us  [on_device(): lax.all_gather(w_query[0], 'dp', axis=1, tiled=True)]
    ppermute x0 -> x7, starting transfers between devices: none -> 17.6 us  [the longest x3 9.33 us: ring_gather(): later.append(lax.ppermute(later[-1], axis, down))]
  transfers between devices with their start and end apart: 14 -> 20, of which waited for: 11 -> 16; matrix products, arithmetic and copies ran while one was open for 10% -> 11% of each run, Pallas kernels for 0% -> 0%
where the time goes in v1:
time: 537 us; the launch traced here: 528 us
  waiting for transfers between devices  370 us (69%)
  matrix products  51.5 us (10%)
  local copies, waits for them, and re-layouts  40.1 us (7%)
  other arithmetic  26 us (5%)
  starting transfers between devices  25.7 us (5%)
  between operations  14.5 us (3%)
    ppermute x4, waiting for transfers between devices, ring_gather(): earlier.append(lax.ppermute(earlier[-1], axis, up))  88 us
    reduce_scatter x3, waiting for transfers between devices, on_device(): lax.psum_scatter(mixed_grad.astype(jnp.bfloat16), 'mp', scatter_dimension...  80.1 us
    all_gather x1, waiting for transfers between devices, on_device(): lax.all_gather(w_key[0], 'dp', axis=1, tiled=True)  66.5 us
    all_gather x2, waiting for transfers between devices, on_device(): full_section = lax.all_gather(own_section, 'mp', axis=1, tiled=True)  41.5 us
    all_gather x1, waiting for transfers between devices, on_device(): lax.all_gather(w_value[0], 'dp', axis=1, tiled=True)  37.7 us
    reduce_scatter x1, waiting for transfers between devices, on_device(): lax.psum_scatter(encoder_partial.astype(jnp.bfloat16), ('segment', 'mp'),...  34.4 us
    another operation x11, local copies, waits for them, and re-layouts  14.8 us
    all_gather x1, waiting for transfers between devices, on_device(): lax.all_gather(w_query[0], 'dp', axis=1, tiled=True)  13.4 us
  transfers between devices with their start and end apart: 20, of which 16 were waited for; matrix products, arithmetic and copies ran while one was open for 11% of the time, Pallas kernels for 0%

profile of v1, /device:TPU:0, one launch (start us, length us, event | category | flops | bytes accessed | tf_op | source)
XLA Modules:
  0.0 528.2 jit_solution(4060708506837453270)
XLA Ops:
  7.9 3.0 collective-permute-start
  10.9 15.4 %collective-permute-done = bf16[1024,256]{1,0:T(8,128)(2,1)S(1)} collective-permute-done((bf16[1024,256]{1,0:T(8,128)(2,1)}, bf16[1024,256]{1,0:T(8,128)(2,1)S(1)}, u32[]{:S(2)}, u32[]{:S(2)}) %collective-permute-start) | collective-permute-done | bytes 524320 | tf_op jit(solution)/shard_map/ppermute | solution.py:18
  26.6 4.4 collective-permute-start.4
  31.0 19.4 %collective-permute-done.1 = bf16[1024,256]{1,0:T(8,128)(2,1)S(1)} collective-permute-done((bf16[1024,256]{1,0:T(8,128)(2,1)S(1)}, bf16[1024,256]{1,0:T(8,128)(2,1)S(1)}, u32[]{:S(2)}, u32[]{:S(2)}) %collective-permute-start.1) | collective-permute-done | bytes 524320 | tf_op jit(solution)/shard_map/ppermute | solution.py:18
  55.9 25.9 %collective-permute-done.2 = bf16[1024,256]{1,0:T(8,128)(2,1)S(1)} collective-permute-done((bf16[1024,256]{1,0:T(8,128)(2,1)S(1)}, bf16[1024,256]{1,0:T(8,128)(2,1)S(1)}, u32[]{:S(2)}, u32[]{:S(2)}) %collective-permute-start.2) | collective-permute-done | bytes 524320 | tf_op jit(solution)/shard_map/ppermute | solution.py:18
  86.8 3.1 collective-permute-start.6
  90.0 27.3 %collective-permute-done.3 = bf16[1024,256]{1,0:T(8,128)(2,1)S(1)} collective-permute-done((bf16[1024,256]{1,0:T(8,128)(2,1)S(1)}, bf16[1024,256]{1,0:T(8,128)(2,1)S(1)}, u32[]{:S(2)}, u32[]{:S(2)}) %collective-permute-start.3) | collective-permute-done | bytes 524320 | tf_op jit(solution)/shard_map/ppermute | solution.py:18
  123.5 13.4 %all-gather.13.cloned.1.call-done = bf16[1,1024,2048]{2,1,0:T(8,128)(2,1)} async-done(((bf16[1,1024,256]{2,1,0:T(8,128)(2,1)}), bf16[1,1024,2048]{2,1,0:T(8,128)(2,1)}) %all-gather.13.cloned.1.call-update) | async-done | bytes 4194320 | tf_op jit(solution)/shard_map/all_gather | solution.py:136
  137.0 3.0 conditional.3
  140.1 46.1 %reduce-scatter.5.cloned.1.call-done = bf16[256,1024]{1,0:T(8,128)(2,1)} async-done(((bf16[256,2048]{1,0:T(8,128)(2,1)}), bf16[256,1024]{1,0:T(8,128)(2,1)}) %reduce-scatter.5.cloned.1.call-update) | async-done | bytes 524304 | tf_op jit(solution)/shard_map/reduce_scatter | solution.py:173
  189.8 21.4 %all-gather.9.cloned.1.call-done = bf16[256,2048]{1,0:T(8,128)(2,1)} async-done(((bf16[256,1024]{1,0:T(8,128)(2,1)}), bf16[256,2048]{1,0:T(8,128)(2,1)}) %all-gather.9.cloned.1.call-update) | async-done | bytes 1048592 | tf_op jit(solution)/shard_map/all_gather | solution.py:181
  212.9 3.1 collective-permute-done.7
  216.1 3.0 dynamic-slice_select_fusion.1
  219.0 31.3 %conditional.4 = (bf16[256,2048]{1,0:T(8,128)(2,1)}, bf16[384,1024]{0,1:T(8,128)(2,1)}, bf16[384,1024]{0,1:T(8,128)(2,1)}) conditional(s32[]{:T(128)} %convert_element_type.206, () %tuple.46, (s32[2,2]{1,0:T(2,128)S(1)}, s32[]{:T(128)}, s32[2,2]{1,0:T(2,128)S(1)}, s32[2,2]{1,0:T(2,128)S(1)}, bf16[1,512,1024]{2,1,0:T(8,128)(2,1)}, ...), branch_computations={%region_7.8_spmd, %region_8.13_spmd} | conditional | flops 3363606528 | bytes 75467568 | solution.py:167
  222.5 3.5 constant_dynamic-slice_fusion.6
  230.5 3.4 fusion.94
  233.9 4.6 convolution_convert_fusion.3
  250.4 20.4 %reduce-scatter.7.cloned.1.call-done = bf16[256,1024]{1,0:T(8,128)(2,1)} async-done(((bf16[256,2048]{1,0:T(8,128)(2,1)}), bf16[256,1024]{1,0:T(8,128)(2,1)}) %reduce-scatter.7.cloned.1.call-update) | async-done | bytes 524304 | tf_op jit(solution)/shard_map/reduce_scatter | solution.py:173
  270.8 2.7 select_dynamic-update-slice_fusion.6
  274.9 20.1 %all-gather.11.cloned.1.call-done = bf16[256,2048]{1,0:T(8,128)(2,1)} async-done(((bf16[256,1024]{1,0:T(8,128)(2,1)}), bf16[256,2048]{1,0:T(8,128)(2,1)}) %all-gather.11.cloned.1.call-update) | async-done | bytes 1048592 | tf_op jit(solution)/shard_map/all_gather | solution.py:181
  303.5 2.8 select_dynamic-update-slice_fusion.1
  307.7 22.9 %conditional.5 = (bf16[256,2048]{1,0:T(8,128)(2,1)}, bf16[384,1024]{0,1:T(8,128)(2,1)}, bf16[384,1024]{0,1:T(8,128)(2,1)}) conditional(s32[]{:T(128)} %convert_element_type.211, () %tuple.48, (s32[2,2]{1,0:T(2,128)S(1)}, s32[]{:T(128)}, s32[2,2]{1,0:T(2,128)S(1)}, s32[2,2]{1,0:T(2,128)S(1)}, bf16[1,512,1024]{2,1,0:T(8,128)(2,1)}, ...), branch_computations={%region_14.15_spmd, %region_15.20_spmd} | conditional | flops 3363606528 | bytes 85953360 | solution.py:167
  311.4 3.1 constant_dynamic-slice_fusion.12
  317.7 3.5 convolution_convert_fusion.5
  330.6 3.5 select_dynamic-update-slice_fusion
  334.1 37.7 %all-gather.17.cloned.1.call-done = bf16[1,1024,2048]{2,1,0:T(8,128)(2,1)} async-done(((bf16[1,1024,256]{2,1,0:T(8,128)(2,1)}), bf16[1,1024,2048]{2,1,0:T(8,128)(2,1)}) %all-gather.17.cloned.1.call-update) | async-done | bytes 4194320 | tf_op jit(solution)/shard_map/all_gather | solution.py:138
  371.9 8.8 %fusion.51 = f32[768,2048]{1,0:T(8,128)} fusion(bf16[768,1024]{0,1:T(8,128)(2,1)} %get-tuple-element.471, bf16[1,1024,2048]{2,1,0:T(8,128)(2,1)} %all-gather.17.cloned.1.call-done), kind=kOutput, calls=%fused_computation.106 | convolution fusion | flops 3221225472 | bytes 12058624 | tf_op jit(solution)/shard_map/dot_general | solution.py:199
  380.7 66.5 %all-gather.15.cloned.1.call-done = bf16[1,1024,2048]{2,1,0:T(8,128)(2,1)} async-done(((bf16[1,1024,256]{2,1,0:T(8,128)(2,1)}), bf16[1,1024,2048]{2,1,0:T(8,128)(2,1)}) %all-gather.15.cloned.1.call-update) | async-done | bytes 4194320 | tf_op jit(solution)/shard_map/all_gather | solution.py:137
  447.1 9.6 %add_convert_fusion = bf16[768,2048]{1,0:T(8,128)(2,1)} fusion(f32[768,2048]{1,0:T(8,128)} %fusion.51, bf16[768,1024]{0,1:T(8,128)(2,1)} %get-tuple-element.472, bf16[1,1024,2048]{2,1,0:T(8,128)(2,1)} %all-gather.15.cloned.1.call-done), kind=kOutput, calls=%fused_computation.105 | convolution fusion | flops 3224371200 | bytes 15204352 | tf_op jit(solution)/shard_map/dot_general | solution.py:199
  458.7 34.4 %reduce-scatter.11.cloned.1.call-done = bf16[768,512]{1,0:T(8,128)(2,1)} async-done(((bf16[768,2048]{1,0:T(8,128)(2,1)}), bf16[768,512]{1,0:T(8,128)(2,1)}) %reduce-scatter.11.cloned.1.call-update) | async-done | bytes 786448 | tf_op jit(solution)/shard_map/reduce_scatter | solution.py:202
  497.6 3.2 collective-permute-start.10
  502.3 13.5 %reduce-scatter.9.cloned.1.call-done = bf16[256,1024]{1,0:T(8,128)(2,1)} async-done(((bf16[256,2048]{1,0:T(8,128)(2,1)}), bf16[256,1024]{1,0:T(8,128)(2,1)}) %reduce-scatter.9.cloned.1.call-update) | async-done | bytes 524304 | tf_op jit(solution)/shard_map/reduce_scatter | solution.py:173
  (177 shorter events, 86.2 us)
Async XLA Ops:
  7.2 129.8 %all-gather.13.cloned.1.call-start = ((), (), s32[]{:S(2)}) async-start(), calls=%async_computation.10 | async-start | bytes 4718592 | tf_op jit(solution)/shard_map/all_gather | solution.py:136
  7.9 178.3 %reduce-scatter.5.cloned.1.call-start = ((), (), s32[]{:S(2)}) async-start(), calls=%async_computation.4 | async-start | bytes 1572864 | tf_op jit(solution)/shard_map/reduce_scatter | solution.py:173
  7.9 18.4 %collective-permute-start = (bf16[1024,256]{1,0:T(8,128)(2,1)}, bf16[1024,256]{1,0:T(8,128)(2,1)S(1)}, u32[]{:S(2)}, u32[]{:S(2)}) collective-permute-start(bf16[1024,256]{1,0:T(8,128)(2,1)} %bitcast.204), channel_id=1, source_target_pairs={{0,2},{2,4},{4,6},{6,8},{8,10},{10,12},{12,14},{14,0},{1,3},{3,5},... | collective-permute-start | bytes 1572872 | tf_op jit(solution)/shard_map/ppermute | solution.py:18
  26.3 24.1 %collective-permute-start.1 = (bf16[1024,256]{1,0:T(8,128)(2,1)S(1)}, bf16[1024,256]{1,0:T(8,128)(2,1)S(1)}, u32[]{:S(2)}, u32[]{:S(2)}) collective-permute-start(bf16[1024,256]{1,0:T(8,128)(2,1)S(1)} %collective-permute-done), channel_id=1, source_target_pairs={{0,2},{2,4},{4,6},{6,8},{8,10},{10,12},{12,14},{14,0},{1,3},{3,5},... | collective-permute-start | bytes 1572872 | tf_op jit(solution)/shard_map/ppermute | solution.py:18
  26.6 27.6 %collective-permute-start.4 = (bf16[1024,256]{1,0:T(8,128)(2,1)}, bf16[1024,256]{1,0:T(8,128)(2,1)S(1)}, u32[]{:S(2)}, u32[]{:S(2)}) collective-permute-start(bf16[1024,256]{1,0:T(8,128)(2,1)} %bitcast.205), channel_id=1, source_target_pairs={{0,14},{2,0},{4,2},{6,4},{8,6},{10,8},{12,10},{14,12},{1,15},{3,1}... | collective-permute-start | bytes 1572872 | tf_op jit(solution)/shard_map/ppermute | solution.py:20
  50.4 31.5 %collective-permute-start.2 = (bf16[1024,256]{1,0:T(8,128)(2,1)S(1)}, bf16[1024,256]{1,0:T(8,128)(2,1)S(1)}, u32[]{:S(2)}, u32[]{:S(2)}) collective-permute-start(bf16[1024,256]{1,0:T(8,128)(2,1)S(1)} %collective-permute-done.1), channel_id=1, source_target_pairs={{0,2},{2,4},{4,6},{6,8},{8,10},{10,12},{12,14},{14,0},{1,3},{3,5},... | collective-permute-start | bytes 1572872 | tf_op jit(solution)/shard_map/ppermute | solution.py:18
  54.2 32.6 %collective-permute-start.5 = (bf16[1024,256]{1,0:T(8,128)(2,1)S(1)}, bf16[1024,256]{1,0:T(8,128)(2,1)S(1)}, u32[]{:S(2)}, u32[]{:S(2)}) collective-permute-start(bf16[1024,256]{1,0:T(8,128)(2,1)S(1)} %collective-permute-done.4), channel_id=1, source_target_pairs={{0,14},{2,0},{4,2},{6,4},{8,6},{10,8},{12,10},{14,12},{1,15},{3,1}... | collective-permute-start | bytes 1572872 | tf_op jit(solution)/shard_map/ppermute | solution.py:20
  81.9 35.4 %collective-permute-start.3 = (bf16[1024,256]{1,0:T(8,128)(2,1)S(1)}, bf16[1024,256]{1,0:T(8,128)(2,1)S(1)}, u32[]{:S(2)}, u32[]{:S(2)}) collective-permute-start(bf16[1024,256]{1,0:T(8,128)(2,1)S(1)} %collective-permute-done.2), channel_id=1, source_target_pairs={{0,2},{2,4},{4,6},{6,8},{8,10},{10,12},{12,14},{14,0},{1,3},{3,5},... | collective-permute-start | bytes 1572872 | tf_op jit(solution)/shard_map/ppermute | solution.py:18
  86.8 33.6 %collective-permute-start.6 = (bf16[1024,256]{1,0:T(8,128)(2,1)S(1)}, bf16[1024,256]{1,0:T(8,128)(2,1)S(1)}, u32[]{:S(2)}, u32[]{:S(2)}) collective-permute-start(bf16[1024,256]{1,0:T(8,128)(2,1)S(1)} %collective-permute-done.5), channel_id=1, source_target_pairs={{0,14},{2,0},{4,2},{6,4},{8,6},{10,8},{12,10},{14,12},{1,15},{3,1}... | collective-permute-start | bytes 1572872 | tf_op jit(solution)/shard_map/ppermute | solution.py:20
  121.0 15.9 %copy-start = (bf16[1,768,1024]{2,1,0:T(8,128)(2,1)S(1)}, bf16[1,768,1024]{2,1,0:T(8,128)(2,1)}, u32[]{:S(2)}) copy-start(bf16[1,768,1024]{2,1,0:T(8,128)(2,1)} %param.20) | copy-start | bytes 4718596
  121.0 15.9 %copy-start.1 = (bf16[1,768,1024]{2,1,0:T(8,128)(2,1)S(1)}, bf16[1,768,1024]{2,1,0:T(8,128)(2,1)}, u32[]{:S(2)}) copy-start(bf16[1,768,1024]{2,1,0:T(8,128)(2,1)} %param.21) | copy-start | bytes 4718596
  121.0 15.9 %copy-start.20 = (s32[2,2]{1,0:T(2,128)S(1)}, s32[2,2]{1,0:T(2,128)}, u32[]{:S(2)}) copy-start(s32[2,2]{1,0:T(2,128)} %param.26) | copy-start | bytes 52
  121.1 15.9 %copy-start.21 = (s32[2,2]{1,0:T(2,128)S(1)}, s32[2,2]{1,0:T(2,128)}, u32[]{:S(2)}) copy-start(s32[2,2]{1,0:T(2,128)} %param.27) | copy-start | bytes 52
  121.1 15.9 %copy-start.22 = (s32[2,2]{1,0:T(2,128)S(1)}, s32[2,2]{1,0:T(2,128)}, u32[]{:S(2)}) copy-start(s32[2,2]{1,0:T(2,128)} %param.28) | copy-start | bytes 52
  140.0 71.1 %all-gather.9.cloned.1.call-start = ((), (), s32[]{:S(2)}) async-start(), calls=%async_computation.5 | async-start | bytes 1572864 | tf_op jit(solution)/shard_map/all_gather | solution.py:181
  189.7 81.1 %reduce-scatter.7.cloned.1.call-start = ((), (), s32[]{:S(2)}) async-start(), calls=%async_computation.6 | async-start | bytes 1572864 | tf_op jit(solution)/shard_map/reduce_scatter | solution.py:173
  211.2 4.9 collective-permute-start.7
  240.6 2.7 copy-start.28
  243.2 3.3 copy-start.25
  250.3 44.6 %all-gather.11.cloned.1.call-start = ((), (), s32[]{:S(2)}) async-start(), calls=%async_computation.7 | async-start | bytes 1572864 | tf_op jit(solution)/shard_map/all_gather | solution.py:181
  273.5 98.4 %all-gather.17.cloned.1.call-start = ((), (), s32[]{:S(2)}) async-start(), calls=%async_computation.12 | async-start | bytes 4718592 | tf_op jit(solution)/shard_map/all_gather | solution.py:138
  274.0 173.1 %all-gather.15.cloned.1.call-start = ((), (), s32[]{:S(2)}) async-start(), calls=%async_computation.11 | async-start | bytes 4718592 | tf_op jit(solution)/shard_map/all_gather | solution.py:137
  274.8 218.3 %reduce-scatter.11.cloned.1.call-start = ((), (), s32[]{:S(2)}) async-start(), calls=%async_computation.9 | async-start | bytes 3932160 | tf_op jit(solution)/shard_map/reduce_scatter | solution.py:202
  294.9 11.4 %collective-permute-start.8 = (bf16[256,2048]{1,0:T(8,128)(2,1)}, bf16[256,2048]{1,0:T(8,128)(2,1)S(1)}, u32[]{:S(2)}, u32[]{:S(2)}) collective-permute-start(bf16[256,2048]{1,0:T(8,128)(2,1)} %all-gather.11.cloned.1.call-done), channel_id=1, source_target_pairs={{16,0},{17,1},{18,2},{19,3},{20,4},{21,5},{22,6},{23,7},{24,8},{25... | collective-permute-start | bytes 3145736 | tf_op jit(solution)/shard_map/ppermute | solution.py:28
  303.5 2.8 copy-start.3
  311.4 3.1 copy-start.2
  456.8 59.0 %reduce-scatter.9.cloned.1.call-start = ((), (), s32[]{:S(2)}) async-start(), calls=%async_computation.8 | async-start | bytes 1572864 | tf_op jit(solution)/shard_map/reduce_scatter | solution.py:173
  495.2 20.6 %copy-start.9 = (bf16[256,2048]{1,0:T(8,128)(2,1)S(1)}, bf16[256,2048]{1,0:T(8,128)(2,1)}, u32[]{:S(2)}) copy-start(bf16[256,2048]{1,0:T(8,128)(2,1)} %dynamic-slice_select_fusion) | copy-start | bytes 3145732
  495.3 22.5 %collective-permute-start.9 = (bf16[256,512]{1,0:T(8,128)(2,1)S(1)}, bf16[256,512]{1,0:T(8,128)(2,1)S(1)}, u32[]{:S(2)}, u32[]{:S(2)}) collective-permute-start(bf16[256,512]{1,0:T(8,128)(2,1)S(1)} %bitcast.231), channel_id=1, source_target_pairs={{0,2},{2,4},{4,6},{6,8},{8,10},{10,12},{12,14},{14,0},{1,3},{3,5},... | collective-permute-start | bytes 786440 | tf_op jit(solution)/shard_map/ppermute | solution.py:37
  497.6 20.5 %collective-permute-start.10 = (bf16[256,512]{1,0:T(8,128)(2,1)}, bf16[256,512]{1,0:T(8,128)(2,1)}, u32[]{:S(2)}, u32[]{:S(2)}) collective-permute-start(bf16[256,512]{1,0:T(8,128)(2,1)} %bitcast.62), channel_id=1, source_target_pairs={{2,0},{4,2},{6,4},{8,6},{10,8},{12,10},{14,12},{0,14},{3,1},{5,3},... | collective-permute-start | bytes 786440 | tf_op jit(solution)/shard_map/ppermute | solution.py:40
  502.3 15.0 %copy-start.4 = (bf16[768,512]{1,0:T(8,128)(2,1)S(1)}, bf16[768,512]{1,0:T(8,128)(2,1)}, u32[]{:S(2)}) copy-start(bf16[768,512]{1,0:T(8,128)(2,1)} %reduce-scatter.11.cloned.1.call-done) | copy-start | bytes 2359300
  517.3 3.0 copy-start.14
  (12 other events, 21.5 us)
Sparse Core Ops, SparseCore 0:
  10.0 126.8 all-gather.12
  140.2 45.9 reduce-scatter.4
  189.8 21.2 all-gather.8
  250.4 20.3 reduce-scatter.6
  273.6 21.2 all-gather.10
  296.8 75.0 all-gather.16
  373.9 73.1 all-gather.14
  456.9 36.1 reduce-scatter.10
  495.4 20.3 reduce-scatter.8
